TPU v7x, 32 devices: a whole 2x2x4 slice. The times are simulated.
32 devices in a mesh: clip: 4 (over y, x), seq: 8 (over z, core).
Axes of the slice: x: 2, y: 2, z: 4, core: 2. Of those that a mesh axis runs over, the one named last changes fastest.
Arguments:
- queries: bfloat16 [16384, 1024], P(('clip', 'seq')), parts along dimension 0, may hold values from -50 to 50
- rgb_kv: bfloat16 [8, 4096, 1024], P('clip', 'seq'), parts along dimension 0, may hold values from -16 to 16
- tile_ids: int32 [128, 8], P(('clip', 'seq')), parts along dimension 0, may hold values from 0 to 31, as said below
- tile_count: int32 [128], P(('clip', 'seq')), parts along dimension 0, may hold values from 2 to 8
- out_weight: bfloat16 [1024, 1024], replicated, may hold values from -0.1875 to 0.1875
- out_grad: bfloat16 [16384, 1024], P(('clip', 'seq')), parts along dimension 0, may hold values from -6 to 6
Outputs:
- joined: bfloat16 [16384, 1024], P(('clip', 'seq')), parts along dimension 0
- d_queries: bfloat16 [16384, 1024], P(('clip', 'seq')), parts along dimension 0
- d_kv: bfloat16 [8, 4096, 1024], P('clip', 'seq'), parts along dimension 0
- d_out_weight: float32 [4096, 1024], P(('clip', 'seq')), parts along dimension 0
There are 4 independent parts, one for each index of `clip`. A program takes and returns all parts, laid end to end along the dimension named above; an argument that names none is the same for every part. Nothing has to cross between parts.
Inputs may be any that keep to these rules, and one draw needn't show every extreme that they name: `tile_ids`: the 4 consecutive blocks of one group name, in their live entries, at most one distinct tile among tiles 4 s to 4 s + 3, for every s. The entries of one list name distinct tiles.
All inputs are finite; a program needn't handle non-finite values.
Results may differ from a plain program's by a relative error of at most 0.015.
Values may be sent and summed in bfloat16 or wider, within the bound.
A program may use at most 192 MiB of HBM per device.

v0:
```python
import functools

import jax
import jax.numpy as jnp
from jax import lax
from jax.experimental import pallas as pl
from jax.experimental.pallas import tpu as pltpu
from jax.sharding import PartitionSpec as P

D = 1024
HEADS = 16
EB = 128
TILE = 128
HEAD_DIM = D // HEADS
PAIR = 2 * HEAD_DIM
CHUNKS = (4, 4)
UNROLL = 2
VMEM_LIMIT = 48 * 1024 * 1024

masked_score = -1e30


def entry_tables(tile_ids, tile_count, tiles_dev, sources):
    entries = tile_ids.shape[1]
    source = tile_ids // tiles_dev
    within = tile_ids % tiles_dev
    usable = jnp.arange(entries)[None, :] < tile_count[:, None]
    matches = (source[:, :, None] == jnp.arange(sources)[None, None, :]) & usable[:, :, None]
    needed = jnp.any(matches, axis=(0, 1))
    wanted = jnp.max(jnp.where(matches, within[:, :, None], 0), axis=(0, 1))
    request = jnp.where(needed, wanted, -1)
    return (source, request)


def gather_kernel(asked_ref, tiles_ref, out_ref):
    out_ref[0] = tiles_ref[:, 0]


def gather_tiles(asked, tiles, first, pairs):
    sources = asked.shape[0]
    width = pairs * PAIR
    return pl.pallas_call(
        gather_kernel,
        grid_spec=pltpu.PrefetchScalarGridSpec(
            num_scalar_prefetch=1,
            grid=(sources,),
            in_specs=[
                pl.BlockSpec(
                    (2, 1, TILE, width),
                    lambda s, asked_ref: (0, jnp.maximum(asked_ref[s], 0), 0, first // pairs),
                )
            ],
            out_specs=pl.BlockSpec((1, 2, TILE, width), lambda s, asked_ref: (s, 0, 0, 0)),
        ),
        out_shape=jax.ShapeDtypeStruct((sources, 2, TILE, width), jnp.bfloat16),
        compiler_params=pltpu.CompilerParams(vmem_limit_bytes=VMEM_LIMIT),
        cost_estimate=pl.CostEstimate(
            flops=0, bytes_accessed=sources * TILE * width * 8, transcendentals=0
        ),
    )(asked, tiles)


def sum_kernel(asked_ref, terms_ref, *rest):
    out_ref, acc = rest[-2:]
    sources = terms_ref.shape[0]
    acc[...] = jnp.zeros_like(acc)

    def step(s, carry):
        asked = asked_ref[s]

        @pl.when(asked >= 0)
        def _():
            for c in range(2):
                acc[c, asked] += terms_ref[s, c].astype(jnp.float32)

        return carry

    lax.fori_loop(0, sources, step, 0)
    out_ref[...] = acc[...].astype(jnp.bfloat16)


def sum_terms(asked, terms, held, tiles_dev, first, pairs):
    sources = asked.shape[0]
    specs = [
        pl.BlockSpec((sources, 2, TILE, PAIR), lambda p, asked_ref: (0, 0, 0, p)),
    ]
    operands = [asked, terms]
    aliases = {}
    if held is not None:
        specs.append(pl.BlockSpec(memory_space=pl.ANY))
        operands.append(held)
        aliases = {2: 0}
    return pl.pallas_call(
        sum_kernel,
        grid_spec=pltpu.PrefetchScalarGridSpec(
            num_scalar_prefetch=1,
            grid=(pairs,),
            in_specs=specs,
            out_specs=pl.BlockSpec(
                (2, tiles_dev, TILE, PAIR), lambda p, asked_ref: (0, 0, 0, first + p)
            ),
            scratch_shapes=[pltpu.VMEM((2, tiles_dev, TILE, PAIR), jnp.float32)],
        ),
        out_shape=jax.ShapeDtypeStruct((2, tiles_dev, TILE, D), jnp.bfloat16),
        input_output_aliases=aliases,
        compiler_params=pltpu.CompilerParams(vmem_limit_bytes=VMEM_LIMIT),
        cost_estimate=pl.CostEstimate(
            flops=sources * TILE * pairs * PAIR * 2,
            bytes_accessed=sources * TILE * pairs * PAIR * 6,
            transcendentals=0,
        ),
    )(*operands)


def dot(a, b):
    return jnp.dot(a, b, preferred_element_type=jnp.float32)


def by_head(transposed):
    row = lax.broadcasted_iota(jnp.int32, (PAIR, EB), 0)
    return jnp.where(row < HEAD_DIM, transposed[:, :EB], transposed[:, EB:])


def attention_kernel(source_ref, count_ref, q_ref, da_ref, kv_ref, *rest):
    att_ref, dq_ref, grads_ref, flipped, scores, sums, qm, qmt, dm, dmt, out_t, dq_t = rest[-12:]
    sources = kv_ref.shape[0]
    blocks = q_ref.shape[0] // EB
    rows_now = UNROLL * TILE
    lane = lax.broadcasted_iota(jnp.int32, (EB, PAIR), 1)
    row = lax.broadcasted_iota(jnp.int32, (PAIR, EB), 0)

    def flip(s, carry):
        for c in range(2):
            flipped[s, c] = kv_ref[s, c].T
        sums[s] = jnp.zeros((2, TILE, PAIR), jnp.float32)
        return carry

    lax.fori_loop(0, sources, flip, 0)

    def spread(block, natural, turned):
        zero = jnp.zeros((EB, PAIR), jnp.bfloat16)
        natural[:EB, :] = jnp.where(lane < HEAD_DIM, block, zero)
        natural[EB:, :] = jnp.where(lane >= HEAD_DIM, block, zero)
        block_t = block.T
        turned[:, :EB] = jnp.where(row < HEAD_DIM, block_t, zero)
        turned[:, EB:] = jnp.where(row >= HEAD_DIM, block_t, zero)

    def one_block(b, carry):
        here = pl.ds(pl.multiple_of(b * EB, EB), EB)
        spread(q_ref[here, :] * jnp.bfloat16(HEAD_DIM**-0.5), qm, qmt)
        spread(da_ref[here, :], dm, dmt)
        count = count_ref[b]
        trips = (count + UNROLL - 1) // UNROLL

        def rows_of(trip):
            return pl.ds(pl.multiple_of(trip * rows_now, rows_now), rows_now)

        def slots_of(trip):
            return [source_ref[b, trip * UNROLL + u] for u in range(UNROLL)]

        def score_step(trip, top):
            for u, slot in enumerate(slots_of(trip)):
                entry = trip * UNROLL + u
                logits = jnp.where(entry < count, dot(kv_ref[slot, 0], qmt[...]), masked_score)
                at = pl.ds(pl.multiple_of(entry * TILE, TILE), TILE)
                scores[at, :] = logits
                top = jnp.maximum(top, jnp.max(logits.reshape(TILE // 8, 8, 2 * EB), axis=0))
            return top

        top = lax.fori_loop(
            0, trips, score_step, jnp.full((8, 2 * EB), masked_score, jnp.float32)
        )
        row_max = jnp.max(top, axis=0, keepdims=True)
        out_t[...] = jnp.zeros_like(out_t)

        def output_step(trip, total):
            at = rows_of(trip)
            terms = jnp.exp(scores[at, :] - row_max)
            scores[at, :] = terms
            values = jnp.concatenate([flipped[s, 1] for s in slots_of(trip)], axis=1)
            out_t[...] += dot(values, terms.astype(jnp.bfloat16))
            return total + jnp.sum(terms.reshape(rows_now // 8, 8, 2 * EB), axis=0)

        total = lax.fori_loop(0, trips, output_step, jnp.zeros((8, 2 * EB), jnp.float32))
        inverse = 1.0 / jnp.sum(total, axis=0, keepdims=True)
        full = out_t[...] * inverse
        att_ref[here, :] = by_head(full).T.astype(jnp.bfloat16)
        delta = jnp.sum(full * dmt[...].astype(jnp.float32), axis=0, keepdims=True)
        dq_t[...] = jnp.zeros_like(dq_t)

        def grad_step(trip, carry):
            at = rows_of(trip)
            slots = slots_of(trip)
            probability = scores[at, :] * inverse
            values = jnp.concatenate([kv_ref[s, 1] for s in slots], axis=0)
            d_weights = dot(values, dmt[...])
            d_scores = (probability * (d_weights - delta)).astype(jnp.bfloat16)
            keys_t = jnp.concatenate([flipped[s, 0] for s in slots], axis=1)
            dq_t[...] += dot(keys_t, d_scores)
            d_keys = dot(d_scores, qm[...])
            d_values = dot(probability.astype(jnp.bfloat16), dm[...])
            for u, slot in enumerate(slots):
                sums[slot, 0] += d_keys[u * TILE : (u + 1) * TILE]
                sums[slot, 1] += d_values[u * TILE : (u + 1) * TILE]
            return carry

        lax.fori_loop(0, trips, grad_step, 0)
        dq_ref[here, :] = (by_head(dq_t[...]).T * HEAD_DIM**-0.5).astype(jnp.bfloat16)
        return carry

    lax.fori_loop(0, blocks, one_block, 0)

    def finish(s, carry):
        grads_ref[s] = sums[s].astype(jnp.bfloat16)
        return carry

    lax.fori_loop(0, sources, finish, 0)


def attention(source, count, queries, d_attended, slots, held, first, pairs):
    sources = slots.shape[0]
    tokens = queries.shape[0]
    entries = source.shape[1]
    columns = pl.BlockSpec((tokens, PAIR), lambda p, *_: (0, first + p))
    chunk = pl.BlockSpec((sources, 2, TILE, PAIR), lambda p, *_: (0, 0, 0, p))
    specs = [columns, columns, chunk]
    operands = [source, count, queries, d_attended, slots]
    aliases = {}
    if held is not None:
        specs += [pl.BlockSpec(memory_space=pl.ANY)] * 2
        operands += list(held)
        aliases = {5: 0, 6: 1}
    whole = jax.ShapeDtypeStruct((tokens, D), jnp.bfloat16)
    products = (tokens // EB) * entries * pairs * TILE * 2 * EB * PAIR * 2 * 6
    return pl.pallas_call(
        attention_kernel,
        grid_spec=pltpu.PrefetchScalarGridSpec(
            num_scalar_prefetch=2,
            grid=(pairs,),
            in_specs=specs,
            out_specs=[columns, columns, chunk],
            scratch_shapes=[
                pltpu.VMEM((sources, 2, TILE, PAIR), jnp.bfloat16),
                pltpu.VMEM((entries * TILE, 2 * EB), jnp.float32),
                pltpu.VMEM((sources, 2, TILE, PAIR), jnp.float32),
                pltpu.VMEM((2 * EB, PAIR), jnp.bfloat16),
                pltpu.VMEM((PAIR, 2 * EB), jnp.bfloat16),
                pltpu.VMEM((2 * EB, PAIR), jnp.bfloat16),
                pltpu.VMEM((PAIR, 2 * EB), jnp.bfloat16),
                pltpu.VMEM((PAIR, 2 * EB), jnp.float32),
                pltpu.VMEM((PAIR, 2 * EB), jnp.float32),
            ],
        ),
        out_shape=[
            whole,
            whole,
            jax.ShapeDtypeStruct((sources, 2, TILE, pairs * PAIR), jnp.bfloat16),
        ],
        input_output_aliases=aliases,
        compiler_params=pltpu.CompilerParams(vmem_limit_bytes=VMEM_LIMIT),
        cost_estimate=pl.CostEstimate(
            flops=products * 4, bytes_accessed=sources * TILE * pairs * PAIR * 8, transcendentals=0
        ),
    )(*operands)


def exchange(array):
    return lax.all_to_all(array, "seq", split_axis=0, concat_axis=0, tiled=True)


def chip_sum(partial, sources):
    core = lax.axis_index("seq") % 2
    parts = partial.reshape(sources // 2, 2, partial.shape[0] // sources, D)
    kept = lax.dynamic_index_in_dim(parts, core, 1, keepdims=False)
    given = lax.dynamic_index_in_dim(parts, 1 - core, 1, keepdims=False).astype(jnp.bfloat16)
    got = lax.ppermute(given, "seq", [(i, i ^ 1) for i in range(sources)])
    return (kept + got.astype(jnp.float32)).astype(jnp.bfloat16)


def chips_sum(chip, sources):
    groups = [list(range(c, sources, 2)) for c in range(2)]
    terms = lax.all_to_all(
        chip, "seq", split_axis=0, concat_axis=0, tiled=True, axis_index_groups=groups
    )
    return jnp.sum(terms.astype(jnp.float32), axis=0)


def local(queries, rgb_kv, tile_ids, tile_count, out_weight, out_grad):
    sources = lax.axis_size("seq")
    tiles_dev = rgb_kv.shape[1] // TILE
    source, request = entry_tables(tile_ids, tile_count, tiles_dev, sources)
    asked = exchange(request[:, None])[:, 0]
    tiles = rgb_kv.reshape(2, tiles_dev, TILE, D)
    starts = [sum(CHUNKS[:i]) for i in range(len(CHUNKS))]
    cuts = list(zip(starts, CHUNKS))
    d_attended = lax.dot_general(
        out_grad, out_weight, (((1,), (1,)), ((), ())), preferred_element_type=jnp.float32
    ).astype(jnp.bfloat16)
    fetched = []
    for first, pairs in cuts:
        outgoing = gather_tiles(asked, tiles, first, pairs)
        if fetched:
            outgoing, d_attended = lax.optimization_barrier((outgoing, d_attended))
        fetched.append(exchange(outgoing))
    held = None
    returned = []
    for (first, pairs), slots in zip(cuts, fetched):
        attended, d_queries, grads = attention(
            source, tile_count, queries, d_attended, slots, held, first, pairs
        )
        if returned:
            attended, grads, returned[-1] = lax.optimization_barrier(
                (attended, grads, returned[-1])
            )
        held = (attended, d_queries)
        returned.append(exchange(grads))
    partial = lax.dot_general(
        attended, out_grad, (((0,), (0,)), ((), ())), preferred_element_type=jnp.float32
    )
    chip = chip_sum(partial, sources)
    chip, returned[-1] = lax.optimization_barrier((chip, returned[-1]))
    d_out_weight = chips_sum(chip, sources)
    joined = dot(attended, out_weight).astype(jnp.bfloat16)
    d_kv = None
    for (first, pairs), terms in zip(cuts, returned):
        d_kv = sum_terms(asked, terms, d_kv, tiles_dev, first, pairs)
    return (joined, d_queries, d_kv.reshape(2, tiles_dev * TILE, D), d_out_weight)


def solution(mesh):
    placed = (
        P(("clip", "seq"), None),
        P("clip", "seq", None),
        P(("clip", "seq"), None),
        P(("clip", "seq")),
        P(),
        P(("clip", "seq"), None),
    )
    return jax.shard_map(
        local,
        mesh=mesh,
        in_specs=placed,
        out_specs=(
            P(("clip", "seq"), None),
            P(("clip", "seq"), None),
            P("clip", "seq", None),
            P(("clip", "seq"), None),
        ),
        check_vma=False,
    )
```

profile of v0, /device:TPU:0, one launch (start us, length us, event | category | flops | bytes accessed | tf_op | source)
XLA Modules:
  0.0 290.5 jit_solution(15027088571590192070)
XLA Ops:
  2.5 11.7 %all_to_all.31 = s32[8,1,1]{2,1,0:T(1,128)S(1)} all-to-all(s32[8,1,1]{2,1,0:T(1,128)S(1)} %copy.15), channel_id=1, replica_groups=mesh['clip'=4,'seq'=8] {'seq'}, dimensions={0} | all-to-all | bytes 64 | tf_op jit(solution)/shard_map/all_to_all | solution.py:268
  14.4 1.6 copy-done.1
  17.1 1.3 copy-done.4
  18.4 4.5 %all-to-all-start.2 = ((bf16[8,2,128,512]{3,2,1,0:T(8,128)(2,1)}), bf16[8,2,128,512]{3,2,1,0:T(8,128)(2,1)}, u32[]{:S(2)}, u32[]{:S(2)}) async-start(bf16[8,2,128,512]{3,2,1,0:T(8,128)(2,1)} %copy-done.4), calls=%async_computation.2 | async-start | bytes 4194304 | tf_op jit(solution)/shard_map/all_to_all | solution.py:268
  22.9 2.3 convolution_convert_fusion.1.da_ref
  27.6 44.4 %all-to-all-done.2.kv_ref = bf16[8,2,128,512]{3,2,1,0:T(8,128)(2,1)} async-done(((bf16[8,2,128,512]{3,2,1,0:T(8,128)(2,1)}), bf16[8,2,128,512]{3,2,1,0:T(8,128)(2,1)}, u32[]{:S(2)}, u32[]{:S(2)}) %all-to-all-start.2) | async-done | bytes 2097184 | tf_op jit(solution)/shard_map/all_to_all | solution.py:268
  72.0 4.3 %all-to-all-start.1 = ((bf16[8,2,128,512]{3,2,1,0:T(8,128)(2,1)}), bf16[8,2,128,512]{3,2,1,0:T(8,128)(2,1)}, u32[]{:S(2)}, u32[]{:S(2)}) async-start(bf16[8,2,128,512]{3,2,1,0:T(8,128)(2,1)} %copy-done.3), calls=%async_computation.1 | async-start | bytes 4194304 | tf_op jit(solution)/shard_map/all_to_all | solution.py:268
  78.8 45.0 %shard_map.95 = (bf16[512,1024]{1,0:T(8,128)(2,1)S(1)}, bf16[512,1024]{1,0:T(8,128)(2,1)}, bf16[8,2,128,512]{3,2,1,0:T(8,128)(2,1)S(1)}) custom-call(s32[4,8]{1,0:T(4,128)S(1)} %get-tuple-element.31.source_ref, s32[4]{0:T(128)S(1)} %copy-done.9, bf16[512,1024]{1,0:T(8,128)(2,1)S(1)} %copy-done.7, bf16[512,1024]{1,0:T(8,128)(2,1)S(1)} %copy-done.10, ...), custom_call_target="tpu_custom_call" | custom-call | flops 25769803776 | bytes 4194304 | tf_op jit(solution)/shard_map/pallas_call | solution.py:235
  123.8 1.3 copy-done.6
  125.4 17.2 %all-to-all-start.3 = ((bf16[8,2,128,512]{3,2,1,0:T(8,128)(2,1)}), bf16[8,2,128,512]{3,2,1,0:T(8,128)(2,1)}, u32[]{:S(2)}, u32[]{:S(2)}) async-start(bf16[8,2,128,512]{3,2,1,0:T(8,128)(2,1)} %copy-done.6), calls=%async_computation.3 | async-start | bytes 4194304 | tf_op jit(solution)/shard_map/all_to_all | solution.py:268
  145.0 45.0 %shard_map.96 = (bf16[512,1024]{1,0:T(8,128)(2,1)S(1)}, bf16[512,1024]{1,0:T(8,128)(2,1)}, bf16[8,2,128,512]{3,2,1,0:T(8,128)(2,1)S(1)}) custom-call(s32[4,8]{1,0:T(4,128)S(1)} %get-tuple-element.31.source_ref, s32[4]{0:T(128)S(1)} %copy-done.9, bf16[512,1024]{1,0:T(8,128)(2,1)S(1)} %copy-done.8, ...), custom_call_target="tpu_custom_call", output_to_operand_aliasing={{0}: (5, {}), {1}: (6, {})} | custom-call | flops 25769803776 | bytes 4194304 | tf_op jit(solution)/shard_map/pallas_call | solution.py:235
  190.0 1.3 copy-done.5
  191.7 17.2 %all-to-all-start.4 = ((bf16[8,2,128,512]{3,2,1,0:T(8,128)(2,1)}), bf16[8,2,128,512]{3,2,1,0:T(8,128)(2,1)}, u32[]{:S(2)}, u32[]{:S(2)}) async-start(bf16[8,2,128,512]{3,2,1,0:T(8,128)(2,1)} %copy-done.5), calls=%async_computation.4 | async-start | bytes 4194304 | tf_op jit(solution)/shard_map/all_to_all | solution.py:268
  208.9 2.5 fusion.5
  211.5 2.0 copy-done.12
  215.0 2.6 collective-permute-done
  217.7 3.3 %fusion = bf16[4,128,1024]{2,1,0:T(8,128)(2,1)} fusion(bf16[4,128,1024]{2,1,0:T(8,128)(2,1)} %collective-permute-done, f32[4,2,128,1024]{3,2,1,0:T(8,128)} %bitcast.20, s32[]{:T(128)S(6)} %select_n.50), kind=kLoop, calls=%fused_computation.1 | loop fusion | flops 1572864 | bytes 4194308 | tf_op jit(solution)/shard_map/convert_element_type | solution.py:277
  221.0 37.1 %all-to-all-done.4.terms_ref = bf16[8,2,128,512]{3,2,1,0:T(8,128)(2,1)} async-done(((bf16[8,2,128,512]{3,2,1,0:T(8,128)(2,1)}), bf16[8,2,128,512]{3,2,1,0:T(8,128)(2,1)}, u32[]{:S(2)}, u32[]{:S(2)}) %all-to-all-start.4) | async-done | bytes 2097184 | tf_op jit(solution)/shard_map/all_to_all | solution.py:268
  258.1 4.2 %all-to-all-start.5 = ((bf16[4,128,1024]{2,1,0:T(8,128)(2,1)}), bf16[4,128,1024]{2,1,0:T(8,128)(2,1)}, u32[]{:S(2)}, u32[]{:S(2)}) async-start(bf16[4,128,1024]{2,1,0:T(8,128)(2,1)} %fusion), calls=%async_computation.5 | async-start | bytes 2097152 | tf_op jit(solution)/shard_map/all_to_all | solution.py:282
  262.3 4.6 %shard_map.97.rest_0_ = bf16[2,4,128,1024]{3,2,1,0:T(8,128)(2,1)} custom-call(s32[8]{0:T(128)S(1)} %reduce.asked_ref, bf16[8,2,128,512]{3,2,1,0:T(8,128)(2,1)} %all-to-all-done.3.terms_ref), custom_call_target="tpu_custom_call" | custom-call | flops 1048576 | bytes 3145728 | tf_op jit(solution)/shard_map/pallas_call | solution.py:93
  266.9 2.2 convolution_convert_fusion
  269.1 4.6 %shard_map.98 = bf16[2,4,128,1024]{3,2,1,0:T(8,128)(2,1)} custom-call(s32[8]{0:T(128)S(1)} %reduce.asked_ref, bf16[8,2,128,512]{3,2,1,0:T(8,128)(2,1)} %all-to-all-done.4.terms_ref, bf16[2,4,128,1024]{3,2,1,0:T(8,128)(2,1)} %shard_map.97.rest_0_), custom_call_target="tpu_custom_call", output_to_operand_aliasing={{}: (2, {})} | custom-call | flops 1048576 | bytes 3145728 | tf_op jit(solution)/shard_map/pallas_call | solution.py:93
  273.7 14.5 %all-to-all-done.5 = bf16[4,128,1024]{2,1,0:T(8,128)(2,1)} async-done(((bf16[4,128,1024]{2,1,0:T(8,128)(2,1)}), bf16[4,128,1024]{2,1,0:T(8,128)(2,1)}, u32[]{:S(2)}, u32[]{:S(2)}) %all-to-all-start.5) | async-done | bytes 1048608 | tf_op jit(solution)/shard_map/all_to_all | solution.py:282
  288.2 2.3 convert_reduce_fusion
  (36 shorter events, 12.7 us)
Async XLA Ops:
  0.6 22.3 %copy-start = (bf16[1024,1024]{1,0:T(8,128)(2,1)S(1)}, bf16[1024,1024]{1,0:T(8,128)(2,1)}, u32[]{:S(2)}) copy-start(bf16[1024,1024]{1,0:T(8,128)(2,1)} %param.10) | copy-start | bytes 6291460
  14.4 1.6 copy-start.1
  17.1 1.3 copy-start.4
  18.4 4.5 %copy-start.13 = (bf16[512,1024]{1,0:T(8,128)(2,1)S(1)}, bf16[512,1024]{1,0:T(8,128)(2,1)}, u32[]{:S(2)}) copy-start(bf16[512,1024]{1,0:T(8,128)(2,1)} %param.11) | copy-start | bytes 3145732
  18.4 53.6 %all-to-all-start.2 = ((bf16[8,2,128,512]{3,2,1,0:T(8,128)(2,1)}), bf16[8,2,128,512]{3,2,1,0:T(8,128)(2,1)}, u32[]{:S(2)}, u32[]{:S(2)}) async-start(bf16[8,2,128,512]{3,2,1,0:T(8,128)(2,1)} %copy-done.4), calls=%async_computation.2 | async-start | bytes 4194304 | tf_op jit(solution)/shard_map/all_to_all | solution.py:268
  22.9 2.3 copy-start.2
  26.3 1.3 copy-start.3
  27.6 48.7 %copy-start.9 = (s32[4]{0:T(128)S(1)}, s32[4]{0:T(128)}, u32[]{:S(2)}) copy-start(s32[4]{0:T(128)} %count_ref.3) | copy-start | bytes 52
  72.0 53.4 %all-to-all-start.1 = ((bf16[8,2,128,512]{3,2,1,0:T(8,128)(2,1)}), bf16[8,2,128,512]{3,2,1,0:T(8,128)(2,1)}, u32[]{:S(2)}, u32[]{:S(2)}) async-start(bf16[8,2,128,512]{3,2,1,0:T(8,128)(2,1)} %copy-done.3), calls=%async_computation.1 | async-start | bytes 4194304 | tf_op jit(solution)/shard_map/all_to_all | solution.py:268
  76.3 1.2 copy-start.7
  77.6 1.2 copy-start.10
  123.8 1.3 copy-start.6
  125.4 66.4 %all-to-all-start.3 = ((bf16[8,2,128,512]{3,2,1,0:T(8,128)(2,1)}), bf16[8,2,128,512]{3,2,1,0:T(8,128)(2,1)}, u32[]{:S(2)}, u32[]{:S(2)}) async-start(bf16[8,2,128,512]{3,2,1,0:T(8,128)(2,1)} %copy-done.6), calls=%async_computation.3 | async-start | bytes 4194304 | tf_op jit(solution)/shard_map/all_to_all | solution.py:268
  142.6 1.2 copy-start.8
  143.8 1.2 copy-start.11
  190.0 1.3 copy-start.5
  191.7 66.4 %all-to-all-start.4 = ((bf16[8,2,128,512]{3,2,1,0:T(8,128)(2,1)}), bf16[8,2,128,512]{3,2,1,0:T(8,128)(2,1)}, u32[]{:S(2)}, u32[]{:S(2)}) async-start(bf16[8,2,128,512]{3,2,1,0:T(8,128)(2,1)} %copy-done.5), calls=%async_computation.4 | async-start | bytes 4194304 | tf_op jit(solution)/shard_map/all_to_all | solution.py:268
  211.4 2.0 copy-start.12
  214.5 3.1 %collective-permute-start = (bf16[4,128,1024]{2,1,0:T(8,128)(2,1)}, bf16[4,128,1024]{2,1,0:T(8,128)(2,1)}, u32[]{:S(2)}, u32[]{:S(2)}) collective-permute-start(bf16[4,128,1024]{2,1,0:T(8,128)(2,1)} %fusion.1), channel_id=1, source_target_pairs={{0,1},{1,0},{2,3},{3,2},{4,5},{5,4},{6,7},{7,6},{8,9},{9,8},{10,11... | collective-permute-start | bytes 3145736 | tf_op jit(solution)/shard_map/ppermute | solution.py:276
  258.1 30.1 %all-to-all-start.5 = ((bf16[4,128,1024]{2,1,0:T(8,128)(2,1)}), bf16[4,128,1024]{2,1,0:T(8,128)(2,1)}, u32[]{:S(2)}, u32[]{:S(2)}) async-start(bf16[4,128,1024]{2,1,0:T(8,128)(2,1)} %fusion), calls=%async_computation.5 | async-start | bytes 2097152 | tf_op jit(solution)/shard_map/all_to_all | solution.py:282
where the time goes:
time: 292 us; the launch traced here: 290 us
  Pallas kernels  101 us (35%)
  waiting for transfers between devices  99.3 us (34%)
  starting transfers between devices  47.9 us (16%)
  local copies, waits for them, and re-layouts  15 us (5%)
  blocking collectives  11.7 us (4%)
  other arithmetic  7.58 us (3%)
  matrix products  6.99 us (2%)
    pallas_call x2, Pallas kernels, attention(): pl.pallas_call(attention_kernel, grid_spec=pltpu.PrefetchScalarGridSpec(n...  90 us
    all_to_all x4, waiting for transfers between devices, exchange(): return lax.all_to_all(array, 'seq', split_axis=0, concat_axis=0, tiled=True)  82.2 us
    all_to_all x4, starting transfers between devices, exchange(): return lax.all_to_all(array, 'seq', split_axis=0, concat_axis=0, tiled=True)  43.2 us
    all_to_all x1, waiting for transfers between devices, chips_sum(): lax.all_to_all(chip, 'seq', split_axis=0, concat_axis=0, tiled=True, axis...  14.5 us
    unnamed x28, local copies, waits for them, and re-layouts  13.8 us
    all_to_all x1, blocking collectives, exchange(): return lax.all_to_all(array, 'seq', split_axis=0, concat_axis=0, tiled=True)  11.7 us
    pallas_call x2, Pallas kernels, sum_terms(): pl.pallas_call(sum_kernel, grid_spec=pltpu.PrefetchScalarGridSpec(num_sca...  9.12 us
  transfers between devices with their start and end apart: 6, of which 6 were waited for; matrix products, arithmetic and copies ran while one was open for 4% of the time, Pallas kernels for 34%

commit v1 on v0

--- a/solution.py
+++ b/solution.py
@@ -14,7 +14,7 @@
 HEAD_DIM = D // HEADS
 PAIR = 2 * HEAD_DIM
 CHUNKS = (4, 4)
-UNROLL = 2
+LOTS = 2
 VMEM_LIMIT = 48 * 1024 * 1024
 
 masked_score = -1e30
@@ -122,10 +122,10 @@
 
 
 def attention_kernel(source_ref, count_ref, q_ref, da_ref, kv_ref, *rest):
-    att_ref, dq_ref, grads_ref, flipped, scores, sums, qm, qmt, dm, dmt, out_t, dq_t = rest[-12:]
+    att_ref, dq_ref, grads_ref, flipped, scores, sums, qm_two, qmt_two, dm_two, dmt_two = rest[-10:]
     sources = kv_ref.shape[0]
     blocks = q_ref.shape[0] // EB
-    rows_now = UNROLL * TILE
+    entries = source_ref.shape[1]
     lane = lax.broadcasted_iota(jnp.int32, (EB, PAIR), 1)
     row = lax.broadcasted_iota(jnp.int32, (PAIR, EB), 0)
 
@@ -135,7 +135,7 @@
         sums[s] = jnp.zeros((2, TILE, PAIR), jnp.float32)
         return carry
 
-    lax.fori_loop(0, sources, flip, 0)
+    lax.fori_loop(0, sources, flip, 0, unroll=4)
 
     def spread(block, natural, turned):
         zero = jnp.zeros((EB, PAIR), jnp.bfloat16)
@@ -145,76 +145,50 @@
         turned[:, :EB] = jnp.where(row < HEAD_DIM, block_t, zero)
         turned[:, EB:] = jnp.where(row >= HEAD_DIM, block_t, zero)
 
-    def one_block(b, carry):
+    def one_block(b, lot):
         here = pl.ds(pl.multiple_of(b * EB, EB), EB)
+        qm, qmt, dm, dmt = (r.at[lot] for r in (qm_two, qmt_two, dm_two, dmt_two))
         spread(q_ref[here, :] * jnp.bfloat16(HEAD_DIM**-0.5), qm, qmt)
         spread(da_ref[here, :], dm, dmt)
         count = count_ref[b]
-        trips = (count + UNROLL - 1) // UNROLL
-
-        def rows_of(trip):
-            return pl.ds(pl.multiple_of(trip * rows_now, rows_now), rows_now)
-
-        def slots_of(trip):
-            return [source_ref[b, trip * UNROLL + u] for u in range(UNROLL)]
-
-        def score_step(trip, top):
-            for u, slot in enumerate(slots_of(trip)):
-                entry = trip * UNROLL + u
-                logits = jnp.where(entry < count, dot(kv_ref[slot, 0], qmt[...]), masked_score)
-                at = pl.ds(pl.multiple_of(entry * TILE, TILE), TILE)
-                scores[at, :] = logits
-                top = jnp.maximum(top, jnp.max(logits.reshape(TILE // 8, 8, 2 * EB), axis=0))
-            return top
-
-        top = lax.fori_loop(
-            0, trips, score_step, jnp.full((8, 2 * EB), masked_score, jnp.float32)
-        )
+        slots = [source_ref[b, j] for j in range(entries)]
+        top = jnp.full((8, 2 * EB), masked_score, jnp.float32)
+        for j, slot in enumerate(slots):
+            logits = jnp.where(j < count, dot(kv_ref[slot, 0], qmt[...]), masked_score)
+            scores[lot, j * TILE : (j + 1) * TILE, :] = logits
+            top = jnp.maximum(top, jnp.max(logits.reshape(TILE // 8, 8, 2 * EB), axis=0))
         row_max = jnp.max(top, axis=0, keepdims=True)
-        out_t[...] = jnp.zeros_like(out_t)
-
-        def output_step(trip, total):
-            at = rows_of(trip)
-            terms = jnp.exp(scores[at, :] - row_max)
-            scores[at, :] = terms
-            values = jnp.concatenate([flipped[s, 1] for s in slots_of(trip)], axis=1)
-            out_t[...] += dot(values, terms.astype(jnp.bfloat16))
-            return total + jnp.sum(terms.reshape(rows_now // 8, 8, 2 * EB), axis=0)
-
-        total = lax.fori_loop(0, trips, output_step, jnp.zeros((8, 2 * EB), jnp.float32))
-        inverse = 1.0 / jnp.sum(total, axis=0, keepdims=True)
-        full = out_t[...] * inverse
+        terms = jnp.exp(scores[lot] - row_max)
+        scores[lot] = terms
+        values = jnp.concatenate([flipped[s, 1] for s in slots], axis=1)
+        out_t = dot(values, terms.astype(jnp.bfloat16))
+        inverse = 1.0 / jnp.sum(terms, axis=0, keepdims=True)
+        full = out_t * inverse
         att_ref[here, :] = by_head(full).T.astype(jnp.bfloat16)
         delta = jnp.sum(full * dmt[...].astype(jnp.float32), axis=0, keepdims=True)
-        dq_t[...] = jnp.zeros_like(dq_t)
-
-        def grad_step(trip, carry):
-            at = rows_of(trip)
-            slots = slots_of(trip)
-            probability = scores[at, :] * inverse
-            values = jnp.concatenate([kv_ref[s, 1] for s in slots], axis=0)
-            d_weights = dot(values, dmt[...])
-            d_scores = (probability * (d_weights - delta)).astype(jnp.bfloat16)
-            keys_t = jnp.concatenate([flipped[s, 0] for s in slots], axis=1)
-            dq_t[...] += dot(keys_t, d_scores)
-            d_keys = dot(d_scores, qm[...])
-            d_values = dot(probability.astype(jnp.bfloat16), dm[...])
-            for u, slot in enumerate(slots):
-                sums[slot, 0] += d_keys[u * TILE : (u + 1) * TILE]
-                sums[slot, 1] += d_values[u * TILE : (u + 1) * TILE]
-            return carry
-
-        lax.fori_loop(0, trips, grad_step, 0)
-        dq_ref[here, :] = (by_head(dq_t[...]).T * HEAD_DIM**-0.5).astype(jnp.bfloat16)
+        probability = scores[lot] * inverse
+        d_weights = dot(jnp.concatenate([kv_ref[s, 1] for s in slots], axis=0), dmt[...])
+        d_scores = (probability * (d_weights - delta)).astype(jnp.bfloat16)
+        dq_t = dot(jnp.concatenate([flipped[s, 0] for s in slots], axis=1), d_scores)
+        d_keys = dot(d_scores, qm[...])
+        d_values = dot(probability.astype(jnp.bfloat16), dm[...])
+        for j, slot in enumerate(slots):
+            sums[slot, 0] += d_keys[j * TILE : (j + 1) * TILE]
+            sums[slot, 1] += d_values[j * TILE : (j + 1) * TILE]
+        dq_ref[here, :] = (by_head(dq_t).T * HEAD_DIM**-0.5).astype(jnp.bfloat16)
+
+    def some_blocks(i, carry):
+        for lot in range(LOTS):
+            one_block(i * LOTS + lot, lot)
         return carry
 
-    lax.fori_loop(0, blocks, one_block, 0)
+    lax.fori_loop(0, blocks // LOTS, some_blocks, 0)
 
     def finish(s, carry):
         grads_ref[s] = sums[s].astype(jnp.bfloat16)
         return carry
 
-    lax.fori_loop(0, sources, finish, 0)
+    lax.fori_loop(0, sources, finish, 0, unroll=4)
 
 
 def attention(source, count, queries, d_attended, slots, held, first, pairs):
@@ -241,14 +215,12 @@
             out_specs=[columns, columns, chunk],
             scratch_shapes=[
                 pltpu.VMEM((sources, 2, TILE, PAIR), jnp.bfloat16),
-                pltpu.VMEM((entries * TILE, 2 * EB), jnp.float32),
+                pltpu.VMEM((LOTS, entries * TILE, 2 * EB), jnp.float32),
                 pltpu.VMEM((sources, 2, TILE, PAIR), jnp.float32),
-                pltpu.VMEM((2 * EB, PAIR), jnp.bfloat16),
-                pltpu.VMEM((PAIR, 2 * EB), jnp.bfloat16),
-                pltpu.VMEM((2 * EB, PAIR), jnp.bfloat16),
-                pltpu.VMEM((PAIR, 2 * EB), jnp.bfloat16),
-                pltpu.VMEM((PAIR, 2 * EB), jnp.float32),
-                pltpu.VMEM((PAIR, 2 * EB), jnp.float32),
+                pltpu.VMEM((LOTS, 2 * EB, PAIR), jnp.bfloat16),
+                pltpu.VMEM((LOTS, PAIR, 2 * EB), jnp.bfloat16),
+                pltpu.VMEM((LOTS, 2 * EB, PAIR), jnp.bfloat16),
+                pltpu.VMEM((LOTS, PAIR, 2 * EB), jnp.bfloat16),
             ],
         ),
         out_shape=[

time: 292 us -> 266 us (0.911)
  Pallas kernels: 101 us -> 65.2 us
  waiting for transfers between devices: 99.3 us -> 135 us
  starting transfers between devices: 47.9 us -> 22.1 us
    pallas_call x2, Pallas kernels: 90 us -> 54.1 us  [attention(): pl.pallas_call(attention_kernel, grid_spec=pltpu.PrefetchScalarGridSpec(n...]
    all_to_all x4, waiting for transfers between devices: 82.2 us -> 118 us  [exchange(): return lax.all_to_all(array, 'seq', split_axis=0, concat_axis=0, tiled=True)]
    all_to_all x4, starting transfers between devices: 43.2 us -> 17.5 us  [exchange(): return lax.all_to_all(array, 'seq', split_axis=0, concat_axis=0, tiled=True)]
  transfers between devices with their start and end apart: 6 -> 6, of which waited for: 6 -> 6; matrix products, arithmetic and copies ran while one was open for 4% -> 4% of each run, Pallas kernels for 34% -> 24%
where the time goes in v1:
time: 266 us; the launch traced here: 265 us
  waiting for transfers between devices  135 us (51%)
  Pallas kernels  65.2 us (25%)
  starting transfers between devices  22.1 us (8%)
  local copies, waits for them, and re-layouts  15 us (6%)
  blocking collectives  11.7 us (4%)
  other arithmetic  7.58 us (3%)
  matrix products  7 us (3%)
    all_to_all x4, waiting for transfers between devices, exchange(): return lax.all_to_all(array, 'seq', split_axis=0, concat_axis=0, tiled=True)  118 us
    pallas_call x2, Pallas kernels, attention(): pl.pallas_call(attention_kernel, grid_spec=pltpu.PrefetchScalarGridSpec(n...  54.1 us
    all_to_all x4, starting transfers between devices, exchange(): return lax.all_to_all(array, 'seq', split_axis=0, concat_axis=0, tiled=True)  17.5 us
    all_to_all x1, waiting for transfers between devices, chips_sum(): lax.all_to_all(chip, 'seq', split_axis=0, concat_axis=0, tiled=True, axis...  14.5 us
    unnamed x28, local copies, waits for them, and re-layouts  13.7 us
    all_to_all x1, blocking collectives, exchange(): return lax.all_to_all(array, 'seq', split_axis=0, concat_axis=0, tiled=True)  11.7 us
    pallas_call x2, Pallas kernels, sum_terms(): pl.pallas_call(sum_kernel, grid_spec=pltpu.PrefetchScalarGridSpec(num_sca...  9.12 us
  transfers between devices with their start and end apart: 6, of which 6 were waited for; matrix products, arithmetic and copies ran while one was open for 4% of the time, Pallas kernels for 24%

profile of v1, /device:TPU:0, one launch (start us, length us, event | category | flops | bytes accessed | tf_op | source)
XLA Modules:
  0.0 264.5 jit_solution(7199270415191123001)
XLA Ops:
  2.5 11.7 %all_to_all.31 = s32[8,1,1]{2,1,0:T(1,128)S(1)} all-to-all(s32[8,1,1]{2,1,0:T(1,128)S(1)} %copy.15), channel_id=1, replica_groups=mesh['clip'=4,'seq'=8] {'seq'}, dimensions={0} | all-to-all | bytes 64 | tf_op jit(solution)/shard_map/all_to_all | solution.py:240
  14.4 1.6 copy-done.1
  18.4 4.5 %all-to-all-start.2 = ((bf16[8,2,128,512]{3,2,1,0:T(8,128)(2,1)}), bf16[8,2,128,512]{3,2,1,0:T(8,128)(2,1)}, u32[]{:S(2)}, u32[]{:S(2)}) async-start(bf16[8,2,128,512]{3,2,1,0:T(8,128)(2,1)} %copy-done.4), calls=%async_computation.2 | async-start | bytes 4194304 | tf_op jit(solution)/shard_map/all_to_all | solution.py:240
  22.9 2.3 convolution_convert_fusion.1.da_ref
  27.5 44.4 %all-to-all-done.2.kv_ref = bf16[8,2,128,512]{3,2,1,0:T(8,128)(2,1)} async-done(((bf16[8,2,128,512]{3,2,1,0:T(8,128)(2,1)}), bf16[8,2,128,512]{3,2,1,0:T(8,128)(2,1)}, u32[]{:S(2)}, u32[]{:S(2)}) %all-to-all-start.2) | async-done | bytes 2097184 | tf_op jit(solution)/shard_map/all_to_all | solution.py:240
  71.9 4.3 %all-to-all-start.1 = ((bf16[8,2,128,512]{3,2,1,0:T(8,128)(2,1)}), bf16[8,2,128,512]{3,2,1,0:T(8,128)(2,1)}, u32[]{:S(2)}, u32[]{:S(2)}) async-start(bf16[8,2,128,512]{3,2,1,0:T(8,128)(2,1)} %copy-done.3), calls=%async_computation.1 | async-start | bytes 4194304 | tf_op jit(solution)/shard_map/all_to_all | solution.py:240
  78.7 27.0 %shard_map.95 = (bf16[512,1024]{1,0:T(8,128)(2,1)S(1)}, bf16[512,1024]{1,0:T(8,128)(2,1)}, bf16[8,2,128,512]{3,2,1,0:T(8,128)(2,1)S(1)}) custom-call(s32[4,8]{1,0:T(4,128)S(1)} %get-tuple-element.31.source_ref, s32[4]{0:T(128)S(1)} %copy-done.9, bf16[512,1024]{1,0:T(8,128)(2,1)S(1)} %copy-done.7, bf16[512,1024]{1,0:T(8,128)(2,1)S(1)} %copy-done.10, ...), custom_call_target="tpu_custom_call" | custom-call | flops 25769803776 | bytes 4194304 | tf_op jit(solution)/shard_map/pallas_call | solution.py:209
  105.8 1.3 copy-done.6
  107.1 18.2 %all-to-all-done.1.kv_ref = bf16[8,2,128,512]{3,2,1,0:T(8,128)(2,1)} async-done(((bf16[8,2,128,512]{3,2,1,0:T(8,128)(2,1)}), bf16[8,2,128,512]{3,2,1,0:T(8,128)(2,1)}, u32[]{:S(2)}, u32[]{:S(2)}) %all-to-all-start.1) | async-done | bytes 2097184 | tf_op jit(solution)/shard_map/all_to_all | solution.py:240
  125.3 4.3 %all-to-all-start.3 = ((bf16[8,2,128,512]{3,2,1,0:T(8,128)(2,1)}), bf16[8,2,128,512]{3,2,1,0:T(8,128)(2,1)}, u32[]{:S(2)}, u32[]{:S(2)}) async-start(bf16[8,2,128,512]{3,2,1,0:T(8,128)(2,1)} %copy-done.6), calls=%async_computation.3 | async-start | bytes 4194304 | tf_op jit(solution)/shard_map/all_to_all | solution.py:240
  132.2 27.0 %shard_map.96 = (bf16[512,1024]{1,0:T(8,128)(2,1)S(1)}, bf16[512,1024]{1,0:T(8,128)(2,1)}, bf16[8,2,128,512]{3,2,1,0:T(8,128)(2,1)S(1)}) custom-call(s32[4,8]{1,0:T(4,128)S(1)} %get-tuple-element.31.source_ref, s32[4]{0:T(128)S(1)} %copy-done.9, bf16[512,1024]{1,0:T(8,128)(2,1)S(1)} %copy-done.8, ...), custom_call_target="tpu_custom_call", output_to_operand_aliasing={{0}: (5, {}), {1}: (6, {})} | custom-call | flops 25769803776 | bytes 4194304 | tf_op jit(solution)/shard_map/pallas_call | solution.py:209
  160.5 18.3 %all-to-all-done.3.terms_ref = bf16[8,2,128,512]{3,2,1,0:T(8,128)(2,1)} async-done(((bf16[8,2,128,512]{3,2,1,0:T(8,128)(2,1)}), bf16[8,2,128,512]{3,2,1,0:T(8,128)(2,1)}, u32[]{:S(2)}, u32[]{:S(2)}) %all-to-all-start.3) | async-done | bytes 2097184 | tf_op jit(solution)/shard_map/all_to_all | solution.py:240
  178.8 4.3 %all-to-all-start.4 = ((bf16[8,2,128,512]{3,2,1,0:T(8,128)(2,1)}), bf16[8,2,128,512]{3,2,1,0:T(8,128)(2,1)}, u32[]{:S(2)}, u32[]{:S(2)}) async-start(bf16[8,2,128,512]{3,2,1,0:T(8,128)(2,1)} %copy-done.5), calls=%async_computation.4 | async-start | bytes 4194304 | tf_op jit(solution)/shard_map/all_to_all | solution.py:240
  183.1 2.5 fusion.5
  185.7 2.0 copy-done.12
  189.1 2.6 %collective-permute-done = bf16[4,128,1024]{2,1,0:T(8,128)(2,1)} collective-permute-done((bf16[4,128,1024]{2,1,0:T(8,128)(2,1)}, bf16[4,128,1024]{2,1,0:T(8,128)(2,1)}, u32[]{:S(2)}, u32[]{:S(2)}) %collective-permute-start) | collective-permute-done | bytes 1048608 | tf_op jit(solution)/shard_map/ppermute | solution.py:248
  191.8 3.3 %fusion = bf16[4,128,1024]{2,1,0:T(8,128)(2,1)} fusion(bf16[4,128,1024]{2,1,0:T(8,128)(2,1)} %collective-permute-done, f32[4,2,128,1024]{3,2,1,0:T(8,128)} %bitcast.20, s32[]{:T(128)S(6)} %select_n.50), kind=kLoop, calls=%fused_computation.1 | loop fusion | flops 1572864 | bytes 4194308 | tf_op jit(solution)/shard_map/convert_element_type | solution.py:249
  195.1 37.1 %all-to-all-done.4.terms_ref = bf16[8,2,128,512]{3,2,1,0:T(8,128)(2,1)} async-done(((bf16[8,2,128,512]{3,2,1,0:T(8,128)(2,1)}), bf16[8,2,128,512]{3,2,1,0:T(8,128)(2,1)}, u32[]{:S(2)}, u32[]{:S(2)}) %all-to-all-start.4) | async-done | bytes 2097184 | tf_op jit(solution)/shard_map/all_to_all | solution.py:240
  232.2 4.2 %all-to-all-start.5 = ((bf16[4,128,1024]{2,1,0:T(8,128)(2,1)}), bf16[4,128,1024]{2,1,0:T(8,128)(2,1)}, u32[]{:S(2)}, u32[]{:S(2)}) async-start(bf16[4,128,1024]{2,1,0:T(8,128)(2,1)} %fusion), calls=%async_computation.5 | async-start | bytes 2097152 | tf_op jit(solution)/shard_map/all_to_all | solution.py:254
  236.4 4.6 %shard_map.97.rest_0_ = bf16[2,4,128,1024]{3,2,1,0:T(8,128)(2,1)} custom-call(s32[8]{0:T(128)S(1)} %reduce.asked_ref, bf16[8,2,128,512]{3,2,1,0:T(8,128)(2,1)} %all-to-all-done.3.terms_ref), custom_call_target="tpu_custom_call" | custom-call | flops 1048576 | bytes 3145728 | tf_op jit(solution)/shard_map/pallas_call | solution.py:93
  241.0 2.2 convolution_convert_fusion
  243.2 4.6 %shard_map.98 = bf16[2,4,128,1024]{3,2,1,0:T(8,128)(2,1)} custom-call(s32[8]{0:T(128)S(1)} %reduce.asked_ref, bf16[8,2,128,512]{3,2,1,0:T(8,128)(2,1)} %all-to-all-done.4.terms_ref, bf16[2,4,128,1024]{3,2,1,0:T(8,128)(2,1)} %shard_map.97.rest_0_), custom_call_target="tpu_custom_call", output_to_operand_aliasing={{}: (2, {})} | custom-call | flops 1048576 | bytes 3145728 | tf_op jit(solution)/shard_map/pallas_call | solution.py:93
  247.8 14.5 %all-to-all-done.5 = bf16[4,128,1024]{2,1,0:T(8,128)(2,1)} async-done(((bf16[4,128,1024]{2,1,0:T(8,128)(2,1)}), bf16[4,128,1024]{2,1,0:T(8,128)(2,1)}, u32[]{:S(2)}, u32[]{:S(2)}) %all-to-all-start.5) | async-done | bytes 1048608 | tf_op jit(solution)/shard_map/all_to_all | solution.py:254
  262.3 2.3 convert_reduce_fusion
  (36 shorter events, 14.5 us)
Async XLA Ops:
  0.6 22.2 %copy-start = (bf16[1024,1024]{1,0:T(8,128)(2,1)S(1)}, bf16[1024,1024]{1,0:T(8,128)(2,1)}, u32[]{:S(2)}) copy-start(bf16[1024,1024]{1,0:T(8,128)(2,1)} %param.10) | copy-start | bytes 6291460
  14.4 1.6 copy-start.1
  17.0 1.3 copy-start.4
  18.4 4.5 %copy-start.13 = (bf16[512,1024]{1,0:T(8,128)(2,1)S(1)}, bf16[512,1024]{1,0:T(8,128)(2,1)}, u32[]{:S(2)}) copy-start(bf16[512,1024]{1,0:T(8,128)(2,1)} %param.11) | copy-start | bytes 3145732
  18.4 53.6 %all-to-all-start.2 = ((bf16[8,2,128,512]{3,2,1,0:T(8,128)(2,1)}), bf16[8,2,128,512]{3,2,1,0:T(8,128)(2,1)}, u32[]{:S(2)}, u32[]{:S(2)}) async-start(bf16[8,2,128,512]{3,2,1,0:T(8,128)(2,1)} %copy-done.4), calls=%async_computation.2 | async-start | bytes 4194304 | tf_op jit(solution)/shard_map/all_to_all | solution.py:240
  22.9 2.3 copy-start.2
  26.2 1.3 copy-start.3
  27.5 48.8 %copy-start.9 = (s32[4]{0:T(128)S(1)}, s32[4]{0:T(128)}, u32[]{:S(2)}) copy-start(s32[4]{0:T(128)} %count_ref.3) | copy-start | bytes 52
  71.9 53.4 %all-to-all-start.1 = ((bf16[8,2,128,512]{3,2,1,0:T(8,128)(2,1)}), bf16[8,2,128,512]{3,2,1,0:T(8,128)(2,1)}, u32[]{:S(2)}, u32[]{:S(2)}) async-start(bf16[8,2,128,512]{3,2,1,0:T(8,128)(2,1)} %copy-done.3), calls=%async_computation.1 | async-start | bytes 4194304 | tf_op jit(solution)/shard_map/all_to_all | solution.py:240
  76.3 1.2 copy-start.7
  77.5 1.2 copy-start.10
  105.8 1.3 copy-start.6
  125.3 53.4 %all-to-all-start.3 = ((bf16[8,2,128,512]{3,2,1,0:T(8,128)(2,1)}), bf16[8,2,128,512]{3,2,1,0:T(8,128)(2,1)}, u32[]{:S(2)}, u32[]{:S(2)}) async-start(bf16[8,2,128,512]{3,2,1,0:T(8,128)(2,1)} %copy-done.6), calls=%async_computation.3 | async-start | bytes 4194304 | tf_op jit(solution)/shard_map/all_to_all | solution.py:240
  129.7 1.2 copy-start.8
  130.9 1.2 copy-start.11
  159.2 1.3 copy-start.5
  178.8 53.4 %all-to-all-start.4 = ((bf16[8,2,128,512]{3,2,1,0:T(8,128)(2,1)}), bf16[8,2,128,512]{3,2,1,0:T(8,128)(2,1)}, u32[]{:S(2)}, u32[]{:S(2)}) async-start(bf16[8,2,128,512]{3,2,1,0:T(8,128)(2,1)} %copy-done.5), calls=%async_computation.4 | async-start | bytes 4194304 | tf_op jit(solution)/shard_map/all_to_all | solution.py:240
  185.7 2.0 copy-start.12
  188.8 3.0 %collective-permute-start = (bf16[4,128,1024]{2,1,0:T(8,128)(2,1)}, bf16[4,128,1024]{2,1,0:T(8,128)(2,1)}, u32[]{:S(2)}, u32[]{:S(2)}) collective-permute-start(bf16[4,128,1024]{2,1,0:T(8,128)(2,1)} %fusion.1), channel_id=1, source_target_pairs={{0,1},{1,0},{2,3},{3,2},{4,5},{5,4},{6,7},{7,6},{8,9},{9,8},{10,11... | collective-permute-start | bytes 3145736 | tf_op jit(solution)/shard_map/ppermute | solution.py:248
  232.2 30.1 %all-to-all-start.5 = ((bf16[4,128,1024]{2,1,0:T(8,128)(2,1)}), bf16[4,128,1024]{2,1,0:T(8,128)(2,1)}, u32[]{:S(2)}, u32[]{:S(2)}) async-start(bf16[4,128,1024]{2,1,0:T(8,128)(2,1)} %fusion), calls=%async_computation.5 | async-start | bytes 2097152 | tf_op jit(solution)/shard_map/all_to_all | solution.py:254

commit v2 on v1

--- a/solution.py
+++ b/solution.py
@@ -250,11 +250,14 @@
 
 
 def chips_sum(chip, sources):
-    groups = [list(range(c, sources, 2)) for c in range(2)]
-    terms = lax.all_to_all(
-        chip, "seq", split_axis=0, concat_axis=0, tiled=True, axis_index_groups=groups
-    )
-    return jnp.sum(terms.astype(jnp.float32), axis=0)
+    chips = sources // 2
+    here = lax.axis_index("seq") // 2
+    total = lax.dynamic_index_in_dim(chip, here, 0, keepdims=False).astype(jnp.float32)
+    for ahead in range(1, chips):
+        piece = lax.dynamic_index_in_dim(chip, (here + ahead) % chips, 0, keepdims=False)
+        route = [(i, (i // 2 + ahead) % chips * 2 + i % 2) for i in range(sources)]
+        total = total + lax.ppermute(piece, "seq", route).astype(jnp.float32)
+    return total
 
 
 def local(queries, rgb_kv, tile_ids, tile_count, out_weight, out_grad):
@@ -290,7 +293,6 @@
         attended, out_grad, (((0,), (0,)), ((), ())), preferred_element_type=jnp.float32
     )
     chip = chip_sum(partial, sources)
-    chip, returned[-1] = lax.optimization_barrier((chip, returned[-1]))
     d_out_weight = chips_sum(chip, sources)
     joined = dot(attended, out_weight).astype(jnp.bfloat16)
     d_kv = None

time: 266 us -> 261 us (0.981)
  other arithmetic: 7.58 us -> 4.52 us
    ppermute x0 -> x3, waiting for transfers between devices: none -> 52.1 us  [chips_sum(): total = total + lax.ppermute(piece, 'seq', route).astype(jnp.float32)]
    all_to_all x4, waiting for transfers between devices: 118 us -> 80.9 us  [exchange(): return lax.all_to_all(array, 'seq', split_axis=0, concat_axis=0, tiled=True)]
    all_to_all x1 -> x0, waiting for transfers between devices: 14.5 us -> none  [chips_sum(): lax.all_to_all(chip, 'seq', split_axis=0, concat_axis=0, tiled=True, axis...]
    ppermute x0 -> x3, starting transfers between devices: none -> 4.68 us  [chips_sum(): total = total + lax.ppermute(piece, 'seq', route).astype(jnp.float32)]
    all_to_all x1 -> x0, starting transfers between devices: 4.24 us -> none  [chips_sum(): lax.all_to_all(chip, 'seq', split_axis=0, concat_axis=0, tiled=True, axis...]
    unnamed x28 -> x30, local copies, waits for them, and re-layouts: 13.7 us -> 13.7 us
  transfers between devices with their start and end apart: 6 -> 8, of which waited for: 6 -> 5; matrix products, arithmetic and copies ran while one was open for 4% -> 4% of each run, Pallas kernels for 24% -> 23%
where the time goes in v2:
time: 261 us; the launch traced here: 260 us
  waiting for transfers between devices  133 us (51%)
  Pallas kernels  65.6 us (25%)
  starting transfers between devices  22.6 us (9%)
  local copies, waits for them, and re-layouts  15 us (6%)
  blocking collectives  11.7 us (4%)
  matrix products  7 us (3%)
  other arithmetic  4.52 us (2%)
    all_to_all x4, waiting for transfers between devices, exchange(): return lax.all_to_all(array, 'seq', split_axis=0, concat_axis=0, tiled=True)  80.9 us
    pallas_call x2, Pallas kernels, attention(): pl.pallas_call(attention_kernel, grid_spec=pltpu.PrefetchScalarGridSpec(n...  54 us
    ppermute x3, waiting for transfers between devices, chips_sum(): total = total + lax.ppermute(piece, 'seq', route).astype(jnp.float32)  52.1 us
    all_to_all x4, starting transfers between devices, exchange(): return lax.all_to_all(array, 'seq', split_axis=0, concat_axis=0, tiled=True)  17.6 us
    unnamed x30, local copies, waits for them, and re-layouts  13.7 us
    all_to_all x1, blocking collectives, exchange(): return lax.all_to_all(array, 'seq', split_axis=0, concat_axis=0, tiled=True)  11.7 us
    pallas_call x2, Pallas kernels, sum_terms(): pl.pallas_call(sum_kernel, grid_spec=pltpu.PrefetchScalarGridSpec(num_sca...  9.4 us
  transfers between devices with their start and end apart: 8, of which 5 were waited for; matrix products, arithmetic and copies ran while one was open for 4% of the time, Pallas kernels for 23%

profile of v2, /device:TPU:0, one launch (start us, length us, event | category | flops | bytes accessed | tf_op | source)
XLA Modules:
  0.0 260.1 jit_solution(15908180937107040707)
XLA Ops:
  2.5 11.7 %all_to_all.26 = s32[8,1,1]{2,1,0:T(1,128)S(1)} all-to-all(s32[8,1,1]{2,1,0:T(1,128)S(1)} %copy.18), channel_id=1, replica_groups=mesh['clip'=4,'seq'=8] {'seq'}, dimensions={0} | all-to-all | bytes 64 | tf_op jit(solution)/shard_map/all_to_all | solution.py:240
  14.4 1.6 copy-done.1
  17.1 1.3 copy-done.4
  18.4 4.5 %all-to-all-start.2 = ((bf16[8,2,128,512]{3,2,1,0:T(8,128)(2,1)}), bf16[8,2,128,512]{3,2,1,0:T(8,128)(2,1)}, u32[]{:S(2)}, u32[]{:S(2)}) async-start(bf16[8,2,128,512]{3,2,1,0:T(8,128)(2,1)} %copy-done.4), calls=%async_computation.2 | async-start | bytes 4194304 | tf_op jit(solution)/shard_map/all_to_all | solution.py:240
  22.9 2.3 convolution_convert_fusion.1.da_ref
  26.3 1.3 copy-done.3
  27.6 44.4 %all-to-all-done.2.kv_ref = bf16[8,2,128,512]{3,2,1,0:T(8,128)(2,1)} async-done(((bf16[8,2,128,512]{3,2,1,0:T(8,128)(2,1)}), bf16[8,2,128,512]{3,2,1,0:T(8,128)(2,1)}, u32[]{:S(2)}, u32[]{:S(2)}) %all-to-all-start.2) | async-done | bytes 2097184 | tf_op jit(solution)/shard_map/all_to_all | solution.py:240
  72.0 4.3 %all-to-all-start.1 = ((bf16[8,2,128,512]{3,2,1,0:T(8,128)(2,1)}), bf16[8,2,128,512]{3,2,1,0:T(8,128)(2,1)}, u32[]{:S(2)}, u32[]{:S(2)}) async-start(bf16[8,2,128,512]{3,2,1,0:T(8,128)(2,1)} %copy-done.3), calls=%async_computation.1 | async-start | bytes 4194304 | tf_op jit(solution)/shard_map/all_to_all | solution.py:240
  78.8 27.0 %shard_map.95 = (bf16[512,1024]{1,0:T(8,128)(2,1)S(1)}, bf16[512,1024]{1,0:T(8,128)(2,1)}, bf16[8,2,128,512]{3,2,1,0:T(8,128)(2,1)S(1)}) custom-call(s32[4,8]{1,0:T(4,128)S(1)} %get-tuple-element.30.source_ref, s32[4]{0:T(128)S(1)} %copy-done.9, bf16[512,1024]{1,0:T(8,128)(2,1)S(1)} %copy-done.7, bf16[512,1024]{1,0:T(8,128)(2,1)S(1)} %copy-done.10, ...), custom_call_target="tpu_custom_call" | custom-call | flops 25769803776 | bytes 4194304 | tf_op jit(solution)/shard_map/pallas_call | solution.py:209
  107.1 18.3 %all-to-all-done.1.kv_ref = bf16[8,2,128,512]{3,2,1,0:T(8,128)(2,1)} async-done(((bf16[8,2,128,512]{3,2,1,0:T(8,128)(2,1)}), bf16[8,2,128,512]{3,2,1,0:T(8,128)(2,1)}, u32[]{:S(2)}, u32[]{:S(2)}) %all-to-all-start.1) | async-done | bytes 2097184 | tf_op jit(solution)/shard_map/all_to_all | solution.py:240
  125.4 4.4 %all-to-all-start.3 = ((bf16[8,2,128,512]{3,2,1,0:T(8,128)(2,1)}), bf16[8,2,128,512]{3,2,1,0:T(8,128)(2,1)}, u32[]{:S(2)}, u32[]{:S(2)}) async-start(bf16[8,2,128,512]{3,2,1,0:T(8,128)(2,1)} %copy-done.6), calls=%async_computation.3 | async-start | bytes 4194304 | tf_op jit(solution)/shard_map/all_to_all | solution.py:240
  132.2 27.0 %shard_map.96 = (bf16[512,1024]{1,0:T(8,128)(2,1)S(1)}, bf16[512,1024]{1,0:T(8,128)(2,1)}, bf16[8,2,128,512]{3,2,1,0:T(8,128)(2,1)S(1)}) custom-call(s32[4,8]{1,0:T(4,128)S(1)} %get-tuple-element.30.source_ref, s32[4]{0:T(128)S(1)} %copy-done.9, bf16[512,1024]{1,0:T(8,128)(2,1)S(1)} %copy-done.8, ...), custom_call_target="tpu_custom_call", output_to_operand_aliasing={{0}: (5, {}), {1}: (6, {})} | custom-call | flops 25769803776 | bytes 4194304 | tf_op jit(solution)/shard_map/pallas_call | solution.py:209
  159.2 1.3 copy-done.5
  160.6 18.2 %all-to-all-done.3.terms_ref = bf16[8,2,128,512]{3,2,1,0:T(8,128)(2,1)} async-done(((bf16[8,2,128,512]{3,2,1,0:T(8,128)(2,1)}), bf16[8,2,128,512]{3,2,1,0:T(8,128)(2,1)}, u32[]{:S(2)}, u32[]{:S(2)}) %all-to-all-start.3) | async-done | bytes 2097184 | tf_op jit(solution)/shard_map/all_to_all | solution.py:240
  178.8 4.4 %all-to-all-start.4 = ((bf16[8,2,128,512]{3,2,1,0:T(8,128)(2,1)}), bf16[8,2,128,512]{3,2,1,0:T(8,128)(2,1)}, u32[]{:S(2)}, u32[]{:S(2)}) async-start(bf16[8,2,128,512]{3,2,1,0:T(8,128)(2,1)} %copy-done.5), calls=%async_computation.4 | async-start | bytes 4194304 | tf_op jit(solution)/shard_map/all_to_all | solution.py:240
  183.2 2.5 fusion.7
  185.7 1.9 copy-done.12
  189.1 4.8 %shard_map.97.rest_0_ = bf16[2,4,128,1024]{3,2,1,0:T(8,128)(2,1)} custom-call(s32[8]{0:T(128)S(1)} %reduce.asked_ref, bf16[8,2,128,512]{3,2,1,0:T(8,128)(2,1)} %all-to-all-done.3.terms_ref), custom_call_target="tpu_custom_call" | custom-call | flops 1048576 | bytes 3145728 | tf_op jit(solution)/shard_map/pallas_call | solution.py:93
  194.0 1.6 fusion
  195.6 3.5 %collective-permute-start.3 = (bf16[128,1024]{1,0:T(8,128)(2,1)S(1)}, bf16[128,1024]{1,0:T(8,128)(2,1)S(1)}, u32[]{:S(2)}, u32[]{:S(2)}) collective-permute-start(bf16[128,1024]{1,0:T(8,128)(2,1)S(1)} %get-tuple-element.27), channel_id=1, source_target_pairs={{0,6},{1,7},{2,0},{3,1},{4,2},{5,3},{6,4},{7,5},{8,14},{9,15},{10,... | collective-permute-start | bytes 786440 | tf_op jit(solution)/shard_map/ppermute | solution.py:259
  200.3 2.2 convolution_convert_fusion
  202.5 21.3 %collective-permute-done.3 = bf16[128,1024]{1,0:T(8,128)(2,1)S(1)} collective-permute-done((bf16[128,1024]{1,0:T(8,128)(2,1)S(1)}, bf16[128,1024]{1,0:T(8,128)(2,1)S(1)}, u32[]{:S(2)}, u32[]{:S(2)}) %collective-permute-start.3) | collective-permute-done | bytes 262176 | tf_op jit(solution)/shard_map/ppermute | solution.py:259
  223.8 30.8 %collective-permute-done.2 = bf16[128,1024]{1,0:T(8,128)(2,1)S(1)} collective-permute-done((bf16[128,1024]{1,0:T(8,128)(2,1)S(1)}, bf16[128,1024]{1,0:T(8,128)(2,1)S(1)}, u32[]{:S(2)}, u32[]{:S(2)}) %collective-permute-start.2) | collective-permute-done | bytes 262176 | tf_op jit(solution)/shard_map/ppermute | solution.py:259
  255.6 4.6 %shard_map.98 = bf16[2,4,128,1024]{3,2,1,0:T(8,128)(2,1)} custom-call(s32[8]{0:T(128)S(1)} %reduce.asked_ref, bf16[8,2,128,512]{3,2,1,0:T(8,128)(2,1)} %all-to-all-done.4.terms_ref, bf16[2,4,128,1024]{3,2,1,0:T(8,128)(2,1)} %shard_map.97.rest_0_), custom_call_target="tpu_custom_call", output_to_operand_aliasing={{}: (2, {})} | custom-call | flops 1048576 | bytes 3145728 | tf_op jit(solution)/shard_map/pallas_call | solution.py:93
  (43 shorter events, 14.1 us)
Async XLA Ops:
  0.6 22.3 %copy-start = (bf16[1024,1024]{1,0:T(8,128)(2,1)S(1)}, bf16[1024,1024]{1,0:T(8,128)(2,1)}, u32[]{:S(2)}) copy-start(bf16[1024,1024]{1,0:T(8,128)(2,1)} %param.10) | copy-start | bytes 6291460
  14.4 1.6 copy-start.1
  17.1 1.3 copy-start.4
  18.4 4.5 %copy-start.14 = (bf16[512,1024]{1,0:T(8,128)(2,1)S(1)}, bf16[512,1024]{1,0:T(8,128)(2,1)}, u32[]{:S(2)}) copy-start(bf16[512,1024]{1,0:T(8,128)(2,1)} %param.11) | copy-start | bytes 3145732
  18.4 53.6 %all-to-all-start.2 = ((bf16[8,2,128,512]{3,2,1,0:T(8,128)(2,1)}), bf16[8,2,128,512]{3,2,1,0:T(8,128)(2,1)}, u32[]{:S(2)}, u32[]{:S(2)}) async-start(bf16[8,2,128,512]{3,2,1,0:T(8,128)(2,1)} %copy-done.4), calls=%async_computation.2 | async-start | bytes 4194304 | tf_op jit(solution)/shard_map/all_to_all | solution.py:240
  22.9 2.3 copy-start.2
  26.3 1.3 copy-start.3
  27.6 48.7 %copy-start.9 = (s32[4]{0:T(128)S(1)}, s32[4]{0:T(128)}, u32[]{:S(2)}) copy-start(s32[4]{0:T(128)} %count_ref.3) | copy-start | bytes 52
  72.0 53.4 %all-to-all-start.1 = ((bf16[8,2,128,512]{3,2,1,0:T(8,128)(2,1)}), bf16[8,2,128,512]{3,2,1,0:T(8,128)(2,1)}, u32[]{:S(2)}, u32[]{:S(2)}) async-start(bf16[8,2,128,512]{3,2,1,0:T(8,128)(2,1)} %copy-done.3), calls=%async_computation.1 | async-start | bytes 4194304 | tf_op jit(solution)/shard_map/all_to_all | solution.py:240
  76.3 1.2 copy-start.7
  77.6 1.2 copy-start.10
  105.8 1.3 copy-start.6
  125.4 53.4 %all-to-all-start.3 = ((bf16[8,2,128,512]{3,2,1,0:T(8,128)(2,1)}), bf16[8,2,128,512]{3,2,1,0:T(8,128)(2,1)}, u32[]{:S(2)}, u32[]{:S(2)}) async-start(bf16[8,2,128,512]{3,2,1,0:T(8,128)(2,1)} %copy-done.6), calls=%async_computation.3 | async-start | bytes 4194304 | tf_op jit(solution)/shard_map/all_to_all | solution.py:240
  129.8 1.2 copy-start.8
  131.0 1.2 copy-start.11
  159.2 1.3 copy-start.5
  178.8 76.8 %all-to-all-start.4 = ((bf16[8,2,128,512]{3,2,1,0:T(8,128)(2,1)}), bf16[8,2,128,512]{3,2,1,0:T(8,128)(2,1)}, u32[]{:S(2)}, u32[]{:S(2)}) async-start(bf16[8,2,128,512]{3,2,1,0:T(8,128)(2,1)} %copy-done.5), calls=%async_computation.4 | async-start | bytes 4194304 | tf_op jit(solution)/shard_map/all_to_all | solution.py:240
  185.7 1.9 copy-start.12
  188.8 5.2 %collective-permute-start = (bf16[4,128,1024]{2,1,0:T(8,128)(2,1)}, bf16[4,128,1024]{2,1,0:T(8,128)(2,1)}, u32[]{:S(2)}, u32[]{:S(2)}) collective-permute-start(bf16[4,128,1024]{2,1,0:T(8,128)(2,1)} %fusion.1), channel_id=1, source_target_pairs={{0,1},{1,0},{2,3},{3,2},{4,5},{5,4},{6,7},{7,6},{8,9},{9,8},{10,11... | collective-permute-start | bytes 3145736 | tf_op jit(solution)/shard_map/ppermute | solution.py:248
  189.1 4.8 %copy-start.13 = (f32[1024,1024]{1,0:T(8,128)S(1)}, f32[1024,1024]{1,0:T(8,128)}, u32[]{:S(2)}) copy-start(f32[1024,1024]{1,0:T(8,128)} %copy-done.12) | copy-start | bytes 12582916
  195.6 28.2 %collective-permute-start.3 = (bf16[128,1024]{1,0:T(8,128)(2,1)S(1)}, bf16[128,1024]{1,0:T(8,128)(2,1)S(1)}, u32[]{:S(2)}, u32[]{:S(2)}) collective-permute-start(bf16[128,1024]{1,0:T(8,128)(2,1)S(1)} %get-tuple-element.27), channel_id=1, source_target_pairs={{0,6},{1,7},{2,0},{3,1},{4,2},{5,3},{6,4},{7,5},{8,14},{9,15},{10,... | collective-permute-start | bytes 786440 | tf_op jit(solution)/shard_map/ppermute | solution.py:259
  199.2 55.4 %collective-permute-start.2 = (bf16[128,1024]{1,0:T(8,128)(2,1)S(1)}, bf16[128,1024]{1,0:T(8,128)(2,1)S(1)}, u32[]{:S(2)}, u32[]{:S(2)}) collective-permute-start(bf16[128,1024]{1,0:T(8,128)(2,1)S(1)} %get-tuple-element.28), channel_id=1, source_target_pairs={{0,4},{1,5},{2,6},{3,7},{4,0},{5,1},{6,2},{7,3},{8,12},{9,13},{10,... | collective-permute-start | bytes 786440 | tf_op jit(solution)/shard_map/ppermute | solution.py:259
  199.2 55.4 %collective-permute-start.1 = (bf16[128,1024]{1,0:T(8,128)(2,1)S(1)}, bf16[128,1024]{1,0:T(8,128)(2,1)S(1)}, u32[]{:S(2)}, u32[]{:S(2)}) collective-permute-start(bf16[128,1024]{1,0:T(8,128)(2,1)S(1)} %get-tuple-element.26), channel_id=1, source_target_pairs={{0,2},{1,3},{2,4},{3,5},{4,6},{5,7},{6,0},{7,1},{8,10},{9,11},{10,... | collective-permute-start | bytes 786440 | tf_op jit(solution)/shard_map/ppermute | solution.py:259
